TPU v7x, 1024 devices: a whole 4x4x32 slice. The times are simulated.
1024 devices in a mesh: group: 8 (over x, core), inner: 128 (over z, y).
Axes of the slice: x: 4, y: 4, z: 32, core: 2. Of those that a mesh axis runs over, the one named last changes fastest.
Arguments:
- out_grad: bfloat16 [2048, 3584], P(('group', 'inner')), may hold values from -6 to 6
- routing_weight: bfloat16 [2048, 8], P(('group', 'inner')), may hold values from 0.099609375 to 1
- expert_ids: int32 [2048, 8], P(('group', 'inner')), may hold values from 0 to 127, as said below
- slot_index: int32 [2048, 8], P(('group', 'inner')), may hold values from 0 to 23, as said below
- w_gate: bfloat16 [3584, 131072], P(None, ('group', 'inner')), may hold values from -0.09375 to 0.09375
- w_up: bfloat16 [3584, 131072], P(None, ('group', 'inner')), may hold values from -0.09375 to 0.09375
- w_down: bfloat16 [131072, 3584], P(('group', 'inner')), may hold values from -0.1875 to 0.1875
- pre_act: bfloat16 [2, 192, 131072], P(None, None, ('group', 'inner')), may hold values from -5 to 5
Outputs:
- grad_tokens: bfloat16 [2048, 3584], P(('group', 'inner'))
- grad_routing: float32 [2048, 8], P(('group', 'inner'))
Inputs may be any that keep to these rules, and one draw needn't show every extreme that they name: `expert_ids`: each token names 8 different experts, two in each of 4 different node groups (expert e lies in group e // 16). Among the 256 tokens of one index of group, every node group is named by exactly half of the tokens, and in every node group half of the experts are named by exactly 24 of these tokens and the other half by 8. slot_index[t, k] is the number of tokens before t, among the 256 tokens of the same index of group, that name expert expert_ids[t, k].
All inputs are finite; a program needn't handle non-finite values.
Results may differ from a plain program's by a relative error of at most 0.0075.
Values may be sent and summed in bfloat16 or wider, within the bound.
A program may use at most 32 MiB of HBM per device.

v0:
```python
import jax
import jax.numpy as jnp
from jax import lax
from jax.sharding import PartitionSpec as P


def expert_backward(token_rows, weight, gate_weight, up_weight, down_weight, saved_pre):
    back_proj = jnp.dot(token_rows, down_weight.T, preferred_element_type=jnp.float32)
    pre_gate = saved_pre[0].astype(jnp.float32)
    pre_up = saved_pre[1].astype(jnp.float32)
    gate_sig = jax.nn.sigmoid(pre_gate)
    swish_gate = pre_gate * gate_sig
    hidden = swish_gate * pre_up
    gate_piece = jnp.sum(hidden * back_proj, axis=1).astype(jnp.bfloat16)
    scaled = weight[:, None] * back_proj
    grad_up = (scaled * swish_gate).astype(jnp.bfloat16)
    grad_gate = (scaled * pre_up * gate_sig * (1.0 + pre_gate * (1.0 - gate_sig))).astype(
        jnp.bfloat16
    )
    partial_value = jnp.dot(grad_gate, gate_weight.T, preferred_element_type=jnp.float32)
    partial_value = partial_value + jnp.dot(
        grad_up, up_weight.T, preferred_element_type=jnp.float32
    )
    return (partial_value.astype(jnp.bfloat16), gate_piece)


def on_device(out_grad, routing_weight, expert_ids, slot_index, w_gate, w_up, w_down, pre_act):
    group_count = lax.axis_size("group")
    inner_count = lax.axis_size("inner")
    split_count = min(8, inner_count // 4)
    experts_here = inner_count // split_count
    inner_index = lax.axis_index("inner")
    local_expert = inner_index // split_count
    block_rows = inner_count * out_grad.shape[0]
    capacity = 3 * block_rows // (2 * experts_here)
    slot_count = group_count * capacity
    model_width = out_grad.shape[1]
    highest = lax.Precision.HIGHEST
    token_rows, token_experts, token_slots, token_weights = (
        lax.all_gather(out_grad, "inner", axis=0, tiled=True),
        lax.all_gather(expert_ids, "inner", axis=0, tiled=True),
        lax.all_gather(slot_index, "inner", axis=0, tiled=True),
        lax.all_gather(routing_weight, "inner", axis=0, tiled=True),
    )
    columns = token_experts // experts_here * capacity + token_slots
    selected = token_experts % experts_here == local_expert
    slot_range = jnp.arange(slot_count, dtype=jnp.int32)
    one_hot = jnp.logical_and(
        columns[:, :, None] == slot_range[None, None, :], selected[:, :, None]
    ).astype(jnp.float32)
    placement_map = jnp.sum(one_hot, axis=1)
    placement_half = placement_map.astype(jnp.bfloat16)
    send_rows = jnp.einsum(
        "ts,td->sd", placement_half, token_rows, preferred_element_type=jnp.float32
    ).astype(jnp.bfloat16)
    send_weight = jnp.einsum(
        "tks,tk->s", one_hot, token_weights.astype(jnp.float32), precision=highest
    ).astype(jnp.bfloat16)
    arrived_rows, arrived_weight = (
        lax.all_to_all(
            send_rows.reshape(group_count, capacity, model_width),
            "group",
            split_axis=0,
            concat_axis=0,
            tiled=True,
        ),
        lax.all_to_all(
            send_weight.reshape(group_count, capacity),
            "group",
            split_axis=0,
            concat_axis=0,
            tiled=True,
        ),
    )
    partial_value, gate_piece = expert_backward(
        arrived_rows.reshape(slot_count, model_width),
        arrived_weight.reshape(slot_count).astype(jnp.float32),
        w_gate,
        w_up,
        w_down,
        pre_act,
    )
    back_rows, back_gate = (
        lax.all_to_all(
            partial_value.reshape(group_count, capacity, model_width),
            "group",
            split_axis=0,
            concat_axis=0,
            tiled=True,
        ),
        lax.all_to_all(
            gate_piece.reshape(group_count, capacity),
            "group",
            split_axis=0,
            concat_axis=0,
            tiled=True,
        ),
    )
    owned_rows = jnp.dot(
        placement_half,
        back_rows.reshape(slot_count, model_width),
        preferred_element_type=jnp.float32,
    )
    gate_share = back_gate.reshape(slot_count).astype(jnp.float32)
    gate_rows = jnp.einsum("tks,s->tk", one_hot, gate_share, precision=highest)
    grad_rows, grad_gate = (
        lax.psum_scatter(owned_rows, "inner", scatter_dimension=0, tiled=True),
        lax.psum_scatter(gate_rows, "inner", scatter_dimension=0, tiled=True),
    )
    return (grad_rows.astype(jnp.bfloat16), grad_gate)


def solution(mesh):
    in_specs = (
        P(("group", "inner"), None),
        P(("group", "inner"), None),
        P(("group", "inner"), None),
        P(("group", "inner"), None),
        P(None, ("group", "inner")),
        P(None, ("group", "inner")),
        P(("group", "inner"), None),
        P(None, None, ("group", "inner")),
    )
    out_specs = (P(("group", "inner"), None), P(("group", "inner"), None))
    return jax.shard_map(
        on_device, mesh=mesh, in_specs=in_specs, out_specs=out_specs, check_vma=False
    )
```

profile of v0, /device:TPU:6, one launch (start us, length us, event | category | flops | bytes accessed | tf_op | source)
XLA Modules:
  0.0 1151.3 jit_solution(7676018709919931318)
XLA Ops:
  7.2 0.0 copy-start
  7.2 0.0 all-gather.6.cloned.1.call-start
  7.2 0.7 all-gather.6.cloned.1.call-update
  7.9 173.3 %all-gather = s32[128,2,8]{2,1,0:T(2,128)S(1)} all-gather(s32[1,2,8]{2,1,0:T(2,128)} %bitcast.53), channel_id=1, replica_groups=mesh['group'=8,'inner'=128] {'inner'}, dimensions={0}, use_global_device_ids=true | all-gather | bytes 8256 | tf_op jit(solution)/shard_map/all_gather | solution.py:41
  181.2 0.1 copy.20
  181.3 158.0 %all-gather.1 = s32[128,2,8]{2,1,0:T(2,128)S(1)} all-gather(s32[1,2,8]{2,1,0:T(2,128)} %bitcast.54), channel_id=1, replica_groups=mesh['group'=8,'inner'=128] {'inner'}, dimensions={0}, use_global_device_ids=true | all-gather | bytes 8256 | tf_op jit(solution)/shard_map/all_gather | solution.py:42
  339.3 0.1 copy.24
  339.3 140.8 %all-gather.2 = bf16[128,2,8]{2,1,0:T(2,128)(2,1)S(1)} all-gather(bf16[1,2,8]{2,1,0:T(2,128)(2,1)} %bitcast.55), channel_id=1, replica_groups=mesh['group'=8,'inner'=128] {'inner'}, dimensions={0}, use_global_device_ids=true | all-gather | bytes 4128 | tf_op jit(solution)/shard_map/all_gather | solution.py:43
  480.2 0.1 copy.27
  480.3 0.4 fusion.4
  480.7 0.7 all_to_all.21
  481.4 4.7 all-to-all-start
  486.1 0.3 convert_reduce_fusion
  486.4 0.0 all-gather.6.cloned.1.call-done
  486.4 4.1 reshape.69
  490.5 1.6 convolution_convert_fusion
  492.1 0.0 copy-start.2
  492.1 0.0 copy-start.3
  492.1 0.0 all-to-all-done
  492.1 4.9 all-to-all-start.1
  497.1 0.1 reshape.59
  497.2 17.3 %all-to-all-done.1 = bf16[8,24,3584]{2,1,0:T(8,128)(2,1)S(1)} async-done(((bf16[8,24,3584]{2,1,0:T(8,128)(2,1)}), bf16[8,24,3584]{2,1,0:T(8,128)(2,1)S(1)}, u32[]{:S(2)}, u32[]{:S(2)}) %all-to-all-start.1) | async-done | bytes 1376288 | tf_op jit(solution)/shard_map/all_to_all | solution.py:60
  514.5 0.0 copy-done.2
  514.5 0.0 copy-done.3
  514.5 0.6 fusion.14
  515.1 0.7 convert_element_type.81
  515.8 5.3 all-to-all-start.3
  521.1 0.0 copy-done
  521.1 0.0 copy-start.1
  521.1 0.6 fusion.19
  521.7 0.6 copy-done.1
  522.3 1.7 fusion
  524.0 0.2 all-to-all-done.3
  524.2 5.6 all-to-all-start.2
  529.8 1.3 dynamic-slice
  531.7 0.1 reshape.72
  531.8 0.4 fusion.2
  532.2 0.1 copy.28
  532.4 14.8 %all-to-all-done.2 = bf16[8,24,3584]{2,1,0:T(8,128)(2,1)S(1)} async-done(((bf16[8,24,3584]{2,1,0:T(8,128)(2,1)}), bf16[8,24,3584]{2,1,0:T(8,128)(2,1)S(1)}, u32[]{:S(2)}, u32[]{:S(2)}) %all-to-all-start.2) | async-done | bytes 1376288 | tf_op jit(solution)/shard_map/all_to_all | solution.py:84
  547.2 2.4 fusion.38
  549.6 592.9 %all-reduce.4 = (bf16[256,3584]{1,0:T(8,128)(2,1)}, f32[256,8]{1,0:T(8,128)S(1)}) all-reduce(f32[256,3584]{1,0:T(8,128)} %fusion.38, f32[256,8]{1,0:T(8,128)S(1)} %bitcast.50), channel_id=2, replica_groups=mesh['group'=8,'inner'=128] {'inner'}, use_global_device_ids=true, to_apply=%region_1.2.clone | all-reduce | flops 919552 | bytes 5521408
  1142.5 1.4 dynamic-slice_convert_fusion
  1143.9 0.6 constant_dynamic-slice_fusion
  (5 shorter events, 0.1 us)
Async XLA Ops:
  7.2 514.0 %copy-start = (bf16[3584,128]{1,0:T(8,128)(2,1)S(1)}, bf16[3584,128]{1,0:T(8,128)(2,1)}, u32[]{:S(2)}) copy-start(bf16[3584,128]{1,0:T(8,128)(2,1)} %param.12) | copy-start | bytes 2752516
  7.2 479.2 %all-gather.6.cloned.1.call-start = ((), (), s32[]{:S(2)}) async-start(), calls=%async_computation.4 | async-start | bytes 1849344 | tf_op jit(solution)/shard_map/all_gather | solution.py:40
  481.4 10.8 all-to-all-start
  492.1 22.4 %copy-start.2 = (bf16[2,192,128]{2,1,0:T(8,128)(2,1)S(1)}, bf16[2,192,128]{2,1,0:T(8,128)(2,1)}, u32[]{:S(2)}) copy-start(bf16[2,192,128]{2,1,0:T(8,128)(2,1)} %param.15) | copy-start | bytes 294916
  492.1 22.4 %copy-start.3 = (bf16[128,3584]{1,0:T(8,128)(2,1)S(1)}, bf16[128,3584]{1,0:T(8,128)(2,1)}, u32[]{:S(2)}) copy-start(bf16[128,3584]{1,0:T(8,128)(2,1)} %param.14) | copy-start | bytes 2752516
  492.1 22.3 %all-to-all-start.1 = ((bf16[8,24,3584]{2,1,0:T(8,128)(2,1)}), bf16[8,24,3584]{2,1,0:T(8,128)(2,1)S(1)}, u32[]{:S(2)}, u32[]{:S(2)}) async-start(bf16[8,24,3584]{2,1,0:T(8,128)(2,1)} %bitcast.45), calls=%async_computation.1 | async-start | bytes 2752512 | tf_op jit(solution)/shard_map/all_to_all | solution.py:60
  515.8 8.4 all-to-all-start.3
  521.1 1.2 copy-start.1
  524.2 23.0 %all-to-all-start.2 = ((bf16[8,24,3584]{2,1,0:T(8,128)(2,1)}), bf16[8,24,3584]{2,1,0:T(8,128)(2,1)S(1)}, u32[]{:S(2)}, u32[]{:S(2)}) async-start(bf16[8,24,3584]{2,1,0:T(8,128)(2,1)} %bitcast.14), calls=%async_computation.2 | async-start | bytes 2752512 | tf_op jit(solution)/shard_map/all_to_all | solution.py:84
Sparse Core Ops, SparseCore 0:
  12.1 273.8 all-gather.5
where the time goes:
time: 1150 us
  blocking collectives  1060 us (92%)
  waiting for transfers between devices  33.1 us (3%)
  starting transfers between devices  20.6 us (2%)
  between operations  14.8 us (1%)
    unnamed x1, blocking collectives  593 us
    all_gather x1, blocking collectives, on_device(): lax.all_gather(expert_ids, 'inner', axis=0, tiled=True)  173 us
    all_gather x1, blocking collectives, on_device(): lax.all_gather(slot_index, 'inner', axis=0, tiled=True)  158 us
    all_gather x1, blocking collectives, on_device(): lax.all_gather(routing_weight, 'inner', axis=0, tiled=True)  141 us
  transfers between devices with their start and end apart: 5, of which 3 were waited for; matrix products, arithmetic and copies ran while one was open for 1% of the time, Pallas kernels for 0%

commit v1 on v0

v1 whole, which is shorter than its diff:
```python
import functools
import jax
import jax.numpy as jnp
from jax import lax
from jax.experimental import pallas as pl
from jax.experimental.pallas import tpu as pltpu
from jax.sharding import PartitionSpec as P

MESH = pl.DeviceIdType.MESH
F32 = jnp.float32
BF16 = jnp.bfloat16
SPLIT = 8
ROWS = 32
META = 64
NT = (((1,), (1,)), ((), ()))
TN = (((0,), (0,)), ((), ()))


def kernel(
    groups, experts, cap,
    grad_ref, weight_ref, ids_ref, slot_ref, wg_hbm, wu_hbm, wd_hbm, pre_hbm,
    out_ref, routing_ref,
    wd_raw, wd_pad, wcat, pre, stage, block_in, block_rows, xbuf, pbuf, wbuf,
    rbuf, ybuf, dbuf, back, gcat, gate, es, eacc, er1, er2, er3, fbuf, vbuf,
    ubuf, gsr, grr, gsl, grl, fin, hbuf,
    load_sem, a_sem, ar_sem, al_sem, b_sem, c_sem, e_sem, f_sem, gr_sem, gl_sem, h_sem,
):
    my_group = lax.axis_index("group")
    my_inner = lax.axis_index("inner")
    le = lax.div(my_inner, SPLIT)
    q = lax.rem(my_inner, SPLIT)
    zp = lax.div(q, 4)
    y = lax.rem(q, 4)
    width = grad_ref.shape[1]
    part = width // SPLIT
    lanes = xbuf.shape[2]
    last = lanes - 128
    half = experts // 2
    slots = groups * cap

    def slot_of(dz, dy):
        return lax.rem(zp + dz, 2) * 4 + lax.rem(y + dy + 4, 4)

    def in_block(index):
        return (my_group, le * SPLIT + index)

    def in_ring(step):
        return (my_group, lax.rem(le + step + experts, experts) * SPLIT + q)

    def in_group(step):
        return (lax.rem(my_group + step, groups), my_inner)

    over_z = in_block(slot_of(1, 0))
    over_up = in_block(slot_of(0, 1))
    over_down = in_block(slot_of(0, -1))
    right, left = in_ring(1), in_ring(-1)

    def send(src, dst, sems, index, target):
        copy = pltpu.make_async_remote_copy(
            src_ref=src, dst_ref=dst, send_sem=sems.at[0, index],
            recv_sem=sems.at[1, index], device_id=target, device_id_type=MESH,
        )
        copy.start()
        started.append(copy)
        return copy

    started = []
    loads = [
        pltpu.make_async_copy(wd_hbm, wd_raw, load_sem.at[0]),
        pltpu.make_async_copy(wg_hbm, wcat.at[pl.ds(0, width), pl.ds(0, 128)], load_sem.at[1]),
        pltpu.make_async_copy(wu_hbm, wcat.at[pl.ds(0, width), pl.ds(128, 128)], load_sem.at[2]),
        pltpu.make_async_copy(pre_hbm, pre, load_sem.at[3]),
    ]
    for load in loads:
        load.start()

    barrier = pltpu.get_barrier_semaphore()
    partners = [in_block(lax.rem(q + d, SPLIT)) for d in range(1, SPLIT)]
    partners += [right, left] + [in_group(d) for d in range(1, groups)]
    for partner in partners:
        pl.semaphore_signal(barrier, inc=1, device_id=partner, device_id_type=MESH)

    lane2 = lax.broadcasted_iota(jnp.int32, (2, 128), 1)
    ids = ids_ref[...]
    local = lax.rem(ids, experts).astype(F32)
    row = (lax.div(ids, experts) * ROWS + slot_ref[...]).astype(F32)
    weight = weight_ref[...].astype(F32)
    meta = jnp.zeros((2, 128), F32)
    for k in range(8):
        for at, values in ((0, local), (8, row), (16, weight)):
            meta = jnp.where(lane2 == META + at + k, values[:, k : k + 1], meta)
    tokens = grad_ref[...].astype(F32)
    for b in range(SPLIT):
        base = part * b // 128 * 128
        cut = tokens[:, base : base + lanes]
        if part * b != base:
            cut = pltpu.roll(cut, lanes - (part * b - base), 1)
        stage[b, :, 0:last] = cut[:, 0:last]
        stage[b, :, last:lanes] = jnp.where(lane2 < META, cut[:, last:lanes], meta)
    block_in[q] = stage[q]

    pl.semaphore_wait(barrier, len(partners))

    copies = []
    for d in range(1, SPLIT):
        target = lax.rem(q + d, SPLIT)
        copies.append(send(stage.at[target], block_in.at[q], a_sem, d - 1, in_block(target)))
    wcat[width:, :] = jnp.zeros((wcat.shape[0] - width, 256), BF16)
    for copy in copies:
        copy.wait_recv()
    for b in range(SPLIT):
        block_rows[2 * b : 2 * b + 2, :] = block_in[b]
    xbuf[le] = block_rows[...].astype(BF16)

    def go_right(k):
        at = lax.rem(le - (k - 1) + experts, experts)
        return send(xbuf.at[at], xbuf.at[at], ar_sem, k - 1, right)

    def go_left(k):
        at = lax.rem(le + (k - 1), experts)
        return send(xbuf.at[at], xbuf.at[at], al_sem, k - 1, left)

    lane_key = lax.broadcasted_iota(jnp.int32, (16, groups * ROWS), 1).astype(F32)
    my_local = le.astype(F32)

    def place(at):
        found = xbuf[at, :, last:lanes].astype(F32)
        key = jnp.where(found == my_local, pltpu.roll(found, 120, 1), -1.0)
        scale = pltpu.roll(found, 112, 1)
        ones = jnp.zeros(lane_key.shape, F32)
        scaled = jnp.zeros(lane_key.shape, F32)
        for k in range(8):
            hit = key[:, META + k : META + k + 1] == lane_key
            ones = jnp.where(hit, 1.0, ones)
            scaled = jnp.where(hit, scale[:, META + k : META + k + 1], scaled)
        pbuf[at] = ones.astype(BF16)
        wbuf[at] = scaled.astype(BF16)

    lane_wd = lax.broadcasted_iota(jnp.int32, (wd_raw.shape[0], lanes), 1)

    def pad_down(b):
        base = part * b // 128 * 128
        cut = wd_raw[:, base : base + lanes].astype(F32)
        if part * b != base:
            cut = pltpu.roll(cut, lanes - (part * b - base), 1)
        wd_pad[b] = jnp.where(lane_wd < part, cut, 0.0).astype(BF16)

    to_right = go_right(1)
    to_left = go_left(1) if half > 1 else None
    place(le)
    loads[0].wait()
    todo = list(range(SPLIT))
    for k in range(1, half + 1):
        to_right.wait_recv()
        if k < half:
            to_right = go_right(k + 1)
            to_left.wait_recv()
            if k < half - 1:
                to_left = go_left(k + 1)
        place(lax.rem(le - k + experts, experts))
        if k < half:
            place(lax.rem(le + k, experts))
            if todo:
                pad_down(todo.pop(0))
    rows = lax.dot_general(
        pbuf[...].reshape(experts * 16, groups * ROWS),
        xbuf[...].reshape(experts * 16, lanes),
        TN, preferred_element_type=F32,
    )
    rbuf[...] = rows.astype(BF16).reshape(rbuf.shape)

    copies = []
    for d in range(1, groups):
        target = lax.rem(my_group + d, groups)
        copies.append(send(rbuf.at[target], ybuf.at[my_group], b_sem, d - 1, in_group(d)))
    ybuf[my_group] = rbuf[my_group]
    while todo:
        pad_down(todo.pop(0))
    for copy in copies:
        copy.wait_recv()
    dense = [ybuf[s].astype(F32)[0:cap] for s in range(groups)]
    dbuf[q] = jnp.concatenate(dense, axis=0).astype(BF16)

    third = slots // 3

    def add_back(dz, dy):
        at = slot_of(dz, dy)
        back[...] += lax.dot_general(dbuf[at], wd_pad[at], NT, preferred_element_type=F32)

    def pass_on(index, dz, dy, target, cut=None):
        view = dbuf.at[slot_of(dz, dy)]
        if cut is not None:
            view = view.at[pl.ds(cut * third, third)]
        return send(view, view, c_sem, index, target)

    z1 = pass_on(0, 0, 0, over_z)
    u1 = pass_on(1, 0, 0, over_up)
    d1 = pass_on(2, 0, 0, over_down)
    back[...] = jnp.zeros(back.shape, F32)
    add_back(0, 0)
    d1.wait_recv()
    z2 = pass_on(3, 0, 1, over_z)
    d2 = pass_on(5, 0, 1, over_down)
    z1.wait_recv()
    u2 = pass_on(4, 1, 0, over_up)
    u1.wait_recv()
    for dz, dy in ((0, 1), (1, 0), (0, -1)):
        add_back(dz, dy)
    d2.wait_recv()
    z3 = pass_on(6, 0, 2, over_z, 0)
    z2.wait_recv()
    d3 = pass_on(8, 1, 1, over_down, 1)
    u2.wait_recv()
    u3 = pass_on(7, 1, -1, over_up, 2)
    for dz, dy in ((0, 2), (1, 1), (1, -1)):
        add_back(dz, dy)
    for load in loads[1:]:
        load.wait()
    z3.wait_recv()
    d3.wait_recv()
    u3.wait_recv()
    add_back(1, 2)

    proj = back[...]
    pre_gate = pre[0].astype(F32)
    pre_up = pre[1].astype(F32)
    sig = jax.nn.sigmoid(pre_gate)
    swish = pre_gate * sig
    gcat[:, 0:128] = (proj * pre_up * sig * (1.0 + pre_gate * (1.0 - sig))).astype(BF16)
    gcat[:, 128:256] = (proj * swish).astype(BF16)
    gate[...] = jnp.broadcast_to(
        jnp.sum(swish * pre_up * proj, axis=1, keepdims=True), gate.shape
    )
    lane_tile = lax.broadcasted_iota(jnp.int32, gate.shape, 1)

    def piece(dz, dy, out, at):
        start = pl.multiple_of(slot_of(dz, dy) * part, 64)
        value = lax.dot_general(
            gcat[...], wcat[pl.ds(start, lanes), :], NT, preferred_element_type=F32
        )
        out[at, :, 0:last] = value[:, 0:last].astype(out.dtype)
        out[at, :, last:lanes] = jnp.where(
            lane_tile < META, value[:, last:lanes], gate[...]
        ).astype(out.dtype)

    piece(1, 2, es, 0)
    z1 = send(es.at[0, pl.ds(0, third)], er1.at[0], e_sem, 0, over_z)
    u1 = send(es.at[0, pl.ds(third, third)], er1.at[1], e_sem, 1, over_up)
    d1 = send(es.at[0, pl.ds(2 * third, third)], er1.at[2], e_sem, 2, over_down)

    def joined(acc, at, arrived, cut):
        piece_at = eacc[acc]
        own = piece_at[cut * third : (cut + 1) * third] + arrived.astype(F32)
        es[at] = piece_at.astype(BF16)
        es[at, cut * third : (cut + 1) * third] = own.astype(BF16)

    piece(1, 1, eacc, 0)
    u1.wait_recv()
    joined(0, 1, er1[1], 1)
    z2 = send(es.at[1], er2.at[0], e_sem, 3, over_z)
    piece(0, 2, eacc, 0)
    z1.wait_recv()
    joined(0, 2, er1[0], 0)
    u2 = send(es.at[2], er2.at[1], e_sem, 4, over_up)
    piece(1, -1, eacc, 0)
    d1.wait_recv()
    joined(0, 3, er1[2], 2)
    d2 = send(es.at[3], er2.at[2], e_sem, 5, over_down)
    piece(0, -1, es, 6)
    d3 = send(es.at[6], er3.at[2], e_sem, 8, over_down)
    piece(1, 0, eacc, 0)
    piece(0, 1, eacc, 1)
    d2.wait_recv()
    es[4] = (eacc[0] + er2[2].astype(F32)).astype(BF16)
    z3 = send(es.at[4], er3.at[0], e_sem, 6, over_z)
    z2.wait_recv()
    u2.wait_recv()
    es[5] = (eacc[1] + er2[0].astype(F32) + er2[1].astype(F32)).astype(BF16)
    u3 = send(es.at[5], er3.at[1], e_sem, 7, over_up)
    piece(0, 0, eacc, 2)
    d3.wait_recv()
    z3.wait_recv()
    u3.wait_recv()
    blank = jnp.zeros((ROWS - cap, lanes), F32)
    summed = (
        eacc[2] + er3[0].astype(F32) + er3[1].astype(F32) + er3[2].astype(F32)
    )
    for s in range(groups):
        fbuf[s] = jnp.concatenate(
            [summed[s * cap : (s + 1) * cap], blank], axis=0
        ).astype(BF16)

    copies = []
    for d in range(1, groups):
        target = lax.rem(my_group + d, groups)
        copies.append(send(fbuf.at[target], vbuf.at[my_group], f_sem, d - 1, in_group(d)))
    vbuf[my_group] = fbuf[my_group]
    for copy in copies:
        copy.wait_recv()

    arrived = vbuf[...].reshape(groups * ROWS, lanes)
    ubuf[...] = lax.dot_general(
        wbuf[...].reshape(experts * 16, groups * ROWS), arrived,
        (((1,), (0,)), ((), ())), preferred_element_type=F32,
    ).reshape(ubuf.shape)
    row_group = lax.div(lax.broadcasted_iota(jnp.int32, (groups * ROWS, 128), 0), ROWS)
    lane_group = lax.broadcasted_iota(jnp.int32, (groups * ROWS, 128), 1) - META
    spread = jnp.where(
        row_group == lane_group, arrived[:, last:lanes].astype(F32), 0.0
    ).astype(BF16)
    terms = lax.dot_general(
        pbuf[...].reshape(experts * 16, groups * ROWS), spread,
        (((1,), (0,)), ((), ())), preferred_element_type=F32,
    )
    found = xbuf[...].reshape(experts * 16, lanes)[:, last:lanes].astype(F32)
    key = jnp.where(found == my_local, pltpu.roll(found, 120, 1), -1.0)
    of_group = jnp.floor(key * (1.0 / ROWS))
    routed = jnp.zeros(found.shape, F32)
    for g in range(groups):
        routed = jnp.where(of_group == g, terms[:, META + g : META + g + 1], routed)
    lane_all = lax.broadcasted_iota(jnp.int32, found.shape, 1)
    mine = ubuf[...].reshape(experts * 16, lanes)[:, last:lanes]
    ubuf[:, :, last:lanes] = jnp.where(lane_all < META, mine, routed).reshape(
        experts, 16, 128
    )

    to_right = to_left = None
    for k in range(1, half + 1):
        value = ubuf[lax.rem(le + half + 1 - k, experts)]
        if to_right is not None:
            to_right.wait_recv()
            value = value + grr[k - 2].astype(F32)
        gsr[k - 1] = value.astype(BF16)
        to_right = send(gsr.at[k - 1], grr.at[k - 1], gr_sem, k - 1, right)
        if k < half:
            value = ubuf[lax.rem(le - (half - k) + experts, experts)]
            if to_left is not None:
                to_left.wait_recv()
                value = value + grl[k - 2].astype(F32)
            gsl[k - 1] = value.astype(BF16)
            to_left = send(gsl.at[k - 1], grl.at[k - 1], gl_sem, k - 1, left)
    value = ubuf[le]
    if to_left is not None:
        to_left.wait_recv()
        value = value + grl[half - 2].astype(F32)
    to_right.wait_recv()
    value = value + grr[half - 1].astype(F32)

    block_rows[...] = value
    for b in range(SPLIT):
        fin[b] = block_rows[2 * b : 2 * b + 2, :]
    hbuf[q] = fin[q]
    copies = []
    for d in range(1, SPLIT):
        target = lax.rem(q + d, SPLIT)
        copies.append(send(fin.at[target], hbuf.at[q], h_sem, d - 1, in_block(target)))
    for copy in copies:
        copy.wait_recv()
    for m in range(SPLIT // 2):
        even = hbuf[2 * m]
        odd = pltpu.roll(hbuf[2 * m + 1], META, 1)
        base = 2 * part * m
        out_ref[:, base : base + last] = even[:, 0:last].astype(BF16)
        out_ref[:, base + last : base + lanes] = jnp.where(
            lane2 < META, even[:, last:lanes], odd[:, 0:128]
        ).astype(BF16)
        out_ref[:, base + lanes : base + 2 * part] = odd[:, 128:lanes].astype(BF16)
    routing_ref[...] = pltpu.roll(hbuf[0][:, last:lanes], 128 - META, 1)[:, 0:8]
    for copy in started:
        copy.wait_send()


def on_device(out_grad, routing_weight, expert_ids, slot_index, w_gate, w_up, w_down, pre_act):
    groups = lax.axis_size("group")
    experts = lax.axis_size("inner") // SPLIT
    cap = pre_act.shape[1] // groups
    width = out_grad.shape[1]
    lanes = -(-(width // SPLIT) // 128) * 128
    slots = groups * cap
    hidden = w_down.shape[0]
    half = experts // 2
    vmem = pltpu.VMEM
    dma = pltpu.SemaphoreType.DMA
    scratch = [
        vmem((hidden, width), BF16),
        vmem((SPLIT, hidden, lanes), BF16),
        vmem((width // SPLIT * (SPLIT - 1) + lanes, 256), BF16),
        vmem((2, slots, hidden), BF16),
        vmem((SPLIT, 2, lanes), F32),
        vmem((SPLIT, 2, lanes), F32),
        vmem((16, lanes), F32),
        vmem((experts, 16, lanes), BF16),
        vmem((experts, 16, groups * ROWS), BF16),
        vmem((experts, 16, groups * ROWS), BF16),
        vmem((groups, ROWS, lanes), BF16),
        vmem((groups, ROWS, lanes), BF16),
        vmem((SPLIT, slots, lanes), BF16),
        vmem((slots, hidden), F32),
        vmem((slots, 256), BF16),
        vmem((slots, 128), F32),
        vmem((7, slots, lanes), BF16),
        vmem((3, slots, lanes), F32),
        vmem((3, slots // 3, lanes), BF16),
        vmem((3, slots, lanes), BF16),
        vmem((3, slots, lanes), BF16),
        vmem((groups, ROWS, lanes), BF16),
        vmem((groups, ROWS, lanes), BF16),
        vmem((experts, 16, lanes), F32),
        vmem((half, 16, lanes), BF16),
        vmem((half, 16, lanes), BF16),
        vmem((half, 16, lanes), BF16),
        vmem((half, 16, lanes), BF16),
        vmem((SPLIT, 2, lanes), F32),
        vmem((SPLIT, 2, lanes), F32),
        dma((4,)),
        dma((2, SPLIT)),
        dma((2, half)),
        dma((2, half)),
        dma((2, groups)),
        dma((2, 9)),
        dma((2, 9)),
        dma((2, groups)),
        dma((2, half)),
        dma((2, half)),
        dma((2, SPLIT)),
    ]
    in_vmem = pl.BlockSpec(memory_space=pltpu.VMEM)
    anywhere = pl.BlockSpec(memory_space=pl.ANY)
    return pl.pallas_call(
        functools.partial(kernel, groups, experts, cap),
        out_shape=(
            jax.ShapeDtypeStruct(out_grad.shape, BF16),
            jax.ShapeDtypeStruct(expert_ids.shape, F32),
        ),
        in_specs=[in_vmem] * 4 + [anywhere] * 4,
        out_specs=(in_vmem, in_vmem),
        scratch_shapes=scratch,
        compiler_params=pltpu.CompilerParams(
            collective_id=0, has_side_effects=True, vmem_limit_bytes=40 * 2**20
        ),
        name="routed_backward",
    )(out_grad, routing_weight, expert_ids, slot_index, w_gate, w_up, w_down, pre_act)


def solution(mesh):
    token = P(("group", "inner"), None)
    in_specs = (
        token, token, token, token,
        P(None, ("group", "inner")),
        P(None, ("group", "inner")),
        P(("group", "inner"), None),
        P(None, None, ("group", "inner")),
    )
    return jax.shard_map(
        on_device, mesh=mesh, in_specs=in_specs, out_specs=(token, token), check_vma=False
    )
```

time: 1150 us -> 138 us (0.12)
  blocking collectives: 1060 us -> 0 us
  Pallas kernels: 0 us -> 128 us
  waiting for transfers between devices: 33.1 us -> 0 us
  starting transfers between devices: 20.6 us -> 0 us
  between operations: 14.8 us -> 0.66 us
    unnamed x1 -> x0, blocking collectives: 593 us -> none
    all_gather x3 -> x0, blocking collectives: 472 us -> none  [the longest x1 173 us: on_device(): lax.all_gather(expert_ids, 'inner', axis=0, tiled=True)]
    pallas_call x0 -> x1, Pallas kernels: none -> 128 us  [on_device(): pl.pallas_call(functools.partial(kernel, groups, experts, cap), out_shape...]
    all_to_all x4 -> x0, waiting for transfers between devices: 32.4 us -> none  [the longest x1 17.3 us: on_device(): lax.all_to_all(send_rows.reshape(group_count, capacity, model_width), 'gr...]
    all_to_all x4 -> x0, starting transfers between devices: 20.6 us -> none  [the longest x1 5.59 us: on_device(): lax.all_to_all(partial_value.reshape(group_count, capacity, model_width),...]
  transfers between devices with their start and end apart: 5 -> 0, of which waited for: 3 -> 0; matrix products, arithmetic and copies ran while one was open for 1% -> 0% of each run, Pallas kernels for 0% -> 0%
where the time goes in v1:
time: 138 us; the launch traced here: 137 us
  Pallas kernels  128 us (93%)
  local copies, waits for them, and re-layouts  8.31 us (6%)
    pallas_call x1, Pallas kernels, on_device(): pl.pallas_call(functools.partial(kernel, groups, experts, cap), out_shape...  128 us
    unnamed x18, local copies, waits for them, and re-layouts  8.31 us

profile of v1, /device:TPU:6, one launch (start us, length us, event | category | flops | bytes accessed | tf_op | source)
XLA Modules:
  0.0 136.9 jit_solution(957935316160504713)
XLA Ops:
  0.6 0.0 copy-start
  0.6 1.2 copy-done
  1.8 0.0 copy-start.1
  1.8 1.2 copy-done.1
  3.0 0.0 copy-start.2
  3.0 1.2 copy-done.2
  4.2 0.0 copy-start.3
  4.2 0.9 copy-done.3
  5.1 0.0 copy-start.4
  5.1 0.7 copy-done.4
  5.8 0.0 copy-start.5
  5.8 0.7 copy-done.5
  6.5 0.0 copy-start.6
  6.5 0.7 copy-done.6
  7.1 0.0 copy-start.7
  7.1 0.7 copy-done.7
  7.8 127.9 %routed_backward.1 = (bf16[2,3584]{1,0:T(2,128)(2,1)S(1)}, f32[2,8]{1,0:T(2,128)S(1)}) custom-call(bf16[2,3584]{1,0:T(2,128)(2,1)S(1)} %copy-done.4, bf16[2,8]{1,0:T(2,128)(2,1)S(1)} %copy-done.7, s32[2,8]{1,0:T(2,128)S(1)} %copy-done.5, s32[2,8]{1,0:T(2,128)S(1)} %copy-done.6, bf16[3584,128]{1,0:T(8,128)(2,1)S(1)} %copy-done, ...), custom_call_target="tpu_custom_call" | custom-call | tf_op jit(solution)/shard_map/routed_backward/pallas_call | solution.py:429
  135.7 0.6 copy.12
  136.3 0.6 copy.13
Async XLA Ops:
  0.6 1.2 copy-start
  1.8 1.2 copy-start.1
  3.0 1.2 copy-start.2
  4.2 0.9 copy-start.3
  5.1 0.7 copy-start.4
  5.8 0.7 copy-start.5
  6.5 0.7 copy-start.6
  7.1 0.7 copy-start.7

commit v2 on v1

--- a/solution.py
+++ b/solution.py
@@ -18,12 +18,13 @@
 
 def kernel(
     groups, experts, cap,
-    grad_ref, weight_ref, ids_ref, slot_ref, wg_hbm, wu_hbm, wd_hbm, pre_hbm,
+    grad_hbm, weight_hbm, ids_hbm, slot_hbm, wg_hbm, wu_hbm, wd_hbm, pre_hbm,
     out_ref, routing_ref,
-    wd_raw, wd_pad, wcat, pre, stage, block_in, block_rows, xbuf, pbuf, wbuf,
+    grad_ref, weight_ref, ids_ref, slot_ref, wd_raw, wd_pad, wcat, pre, stage, block_in, block_rows, xbuf, pbuf, wbuf,
     rbuf, ybuf, dbuf, back, gcat, gate, es, eacc, er1, er2, er3, fbuf, vbuf,
-    ubuf, gsr, grr, gsl, grl, fin, hbuf,
-    load_sem, a_sem, ar_sem, al_sem, b_sem, c_sem, e_sem, f_sem, gr_sem, gl_sem, h_sem,
+    ubuf, ubf, gsr, grr, gsl, grl, gnr, gnl, fin, hbuf,
+    load_sem, a_sem, ar_sem, al_sem, anr_sem, anl_sem, b_sem, c_sem, e_sem, f_sem,
+    gr_sem, gl_sem, gnr_sem, gnl_sem, h_sem,
 ):
     my_group = lax.axis_index("group")
     my_inner = lax.axis_index("inner")
@@ -35,7 +36,7 @@
     part = width // SPLIT
     lanes = xbuf.shape[2]
     last = lanes - 128
-    half = experts // 2
+    half = experts // 4
     slots = groups * cap
 
     def slot_of(dz, dy):
@@ -53,7 +54,8 @@
     over_z = in_block(slot_of(1, 0))
     over_up = in_block(slot_of(0, 1))
     over_down = in_block(slot_of(0, -1))
-    right, left = in_ring(1), in_ring(-1)
+    right, left = in_ring(2), in_ring(-2)
+    next_right, next_left = in_ring(1), in_ring(-1)
 
     def send(src, dst, sems, index, target):
         copy = pltpu.make_async_remote_copy(
@@ -71,15 +73,23 @@
         pltpu.make_async_copy(wu_hbm, wcat.at[pl.ds(0, width), pl.ds(128, 128)], load_sem.at[2]),
         pltpu.make_async_copy(pre_hbm, pre, load_sem.at[3]),
     ]
-    for load in loads:
+    small = [
+        pltpu.make_async_copy(grad_hbm, grad_ref, load_sem.at[4]),
+        pltpu.make_async_copy(weight_hbm, weight_ref, load_sem.at[5]),
+        pltpu.make_async_copy(ids_hbm, ids_ref, load_sem.at[6]),
+        pltpu.make_async_copy(slot_hbm, slot_ref, load_sem.at[7]),
+    ]
+    for load in small + loads:
         load.start()
 
     barrier = pltpu.get_barrier_semaphore()
     partners = [in_block(lax.rem(q + d, SPLIT)) for d in range(1, SPLIT)]
-    partners += [right, left] + [in_group(d) for d in range(1, groups)]
+    partners += [right, left, next_right, next_left] + [in_group(d) for d in range(1, groups)]
     for partner in partners:
         pl.semaphore_signal(barrier, inc=1, device_id=partner, device_id_type=MESH)
 
+    for load in small:
+        load.wait()
     lane2 = lax.broadcasted_iota(jnp.int32, (2, 128), 1)
     ids = ids_ref[...]
     local = lax.rem(ids, experts).astype(F32)
@@ -112,13 +122,11 @@
         block_rows[2 * b : 2 * b + 2, :] = block_in[b]
     xbuf[le] = block_rows[...].astype(BF16)
 
-    def go_right(k):
-        at = lax.rem(le - (k - 1) + experts, experts)
-        return send(xbuf.at[at], xbuf.at[at], ar_sem, k - 1, right)
-
-    def go_left(k):
-        at = lax.rem(le + (k - 1), experts)
-        return send(xbuf.at[at], xbuf.at[at], al_sem, k - 1, left)
+    def block(step):
+        return lax.rem(le + step + experts, experts)
+
+    def go(step, sems, index, target):
+        return send(xbuf.at[block(step)], xbuf.at[block(step)], sems, index, target)
 
     lane_key = lax.broadcasted_iota(jnp.int32, (16, groups * ROWS), 1).astype(F32)
     my_local = le.astype(F32)
@@ -145,22 +153,31 @@
             cut = pltpu.roll(cut, lanes - (part * b - base), 1)
         wd_pad[b] = jnp.where(lane_wd < part, cut, 0.0).astype(BF16)
 
-    to_right = go_right(1)
-    to_left = go_left(1) if half > 1 else None
+    to_right = go(0, ar_sem, 0, right)
+    to_left = go(0, al_sem, 0, left) if half > 1 else None
+    near_right = go(0, anr_sem, 0, next_right)
+    near_left = go(0, anl_sem, 0, next_left)
     place(le)
     loads[0].wait()
     todo = list(range(SPLIT))
     for k in range(1, half + 1):
+        last_right, last_left = near_right, near_left
+        if k < half:
+            to_left.wait_recv()
+            if k < half - 1:
+                to_left = go(2 * k, al_sem, k, left)
+            near_left = go(2 * k, anl_sem, k, next_left)
         to_right.wait_recv()
         if k < half:
-            to_right = go_right(k + 1)
-            to_left.wait_recv()
-            if k < half - 1:
-                to_left = go_left(k + 1)
-        place(lax.rem(le - k + experts, experts))
-        if k < half:
-            place(lax.rem(le + k, experts))
-            if todo:
+            to_right = go(-2 * k, ar_sem, k, right)
+            near_right = go(-2 * k, anr_sem, k, next_right)
+            place(block(2 * k))
+        last_right.wait_recv()
+        last_left.wait_recv()
+        for step in (1 - 2 * k, 2 * k - 1, -2 * k):
+            place(block(step))
+        for _ in range(2):
+            if todo and k < half:
                 pad_down(todo.pop(0))
     rows = lax.dot_general(
         pbuf[...].reshape(experts * 16, groups * ROWS),
@@ -324,22 +341,32 @@
         experts, 16, 128
     )
 
-    to_right = to_left = None
-    for k in range(1, half + 1):
-        value = ubuf[lax.rem(le + half + 1 - k, experts)]
-        if to_right is not None:
-            to_right.wait_recv()
-            value = value + grr[k - 2].astype(F32)
-        gsr[k - 1] = value.astype(BF16)
-        to_right = send(gsr.at[k - 1], grr.at[k - 1], gr_sem, k - 1, right)
-        if k < half:
-            value = ubuf[lax.rem(le - (half - k) + experts, experts)]
-            if to_left is not None:
-                to_left.wait_recv()
-                value = value + grl[k - 2].astype(F32)
-            gsl[k - 1] = value.astype(BF16)
-            to_left = send(gsl.at[k - 1], grl.at[k - 1], gl_sem, k - 1, left)
-    value = ubuf[le]
+    ubf[...] = ubuf[...].astype(BF16)
+    to_right = send(ubf.at[block(2 * half)], grr.at[0], gr_sem, 0, right)
+    to_left = None
+    near_right, near_left = [None] * half, [None] * half
+    for k in range(half - 1, -1, -1):
+        near_left[k] = send(ubf.at[block(-1 - 2 * k)], gnl.at[k], gnl_sem, k, next_left)
+        near_right[k] = send(ubf.at[block(1 + 2 * k)], gnr.at[k], gnr_sem, k, next_right)
+    for k in range(half - 1, 0, -1):
+        value = ubuf[block(-2 * k)]
+        near_left[k].wait_recv()
+        value = value + gnl[k].astype(F32)
+        if to_left is not None:
+            to_left.wait_recv()
+            value = value + grl[half - 2 - k].astype(F32)
+        gsl[half - 1 - k] = value.astype(BF16)
+        to_left = send(gsl.at[half - 1 - k], grl.at[half - 1 - k], gl_sem, half - 1 - k, left)
+        value = ubuf[block(2 * k)]
+        near_right[k].wait_recv()
+        value = value + gnr[k].astype(F32)
+        to_right.wait_recv()
+        value = value + grr[half - 1 - k].astype(F32)
+        gsr[half - 1 - k] = value.astype(BF16)
+        to_right = send(gsr.at[half - 1 - k], grr.at[half - k], gr_sem, half - k, right)
+    near_right[0].wait_recv()
+    near_left[0].wait_recv()
+    value = ubuf[le] + gnr[0].astype(F32) + gnl[0].astype(F32)
     if to_left is not None:
         to_left.wait_recv()
         value = value + grl[half - 2].astype(F32)
@@ -378,10 +405,14 @@
     lanes = -(-(width // SPLIT) // 128) * 128
     slots = groups * cap
     hidden = w_down.shape[0]
-    half = experts // 2
+    half = experts // 4
     vmem = pltpu.VMEM
     dma = pltpu.SemaphoreType.DMA
     scratch = [
+        vmem(out_grad.shape, BF16),
+        vmem(routing_weight.shape, BF16),
+        vmem(expert_ids.shape, jnp.int32),
+        vmem(slot_index.shape, jnp.int32),
         vmem((hidden, width), BF16),
         vmem((SPLIT, hidden, lanes), BF16),
         vmem((width // SPLIT * (SPLIT - 1) + lanes, 256), BF16),
@@ -406,20 +437,27 @@
         vmem((groups, ROWS, lanes), BF16),
         vmem((groups, ROWS, lanes), BF16),
         vmem((experts, 16, lanes), F32),
+        vmem((experts, 16, lanes), BF16),
+        vmem((half, 16, lanes), BF16),
+        vmem((half, 16, lanes), BF16),
         vmem((half, 16, lanes), BF16),
         vmem((half, 16, lanes), BF16),
         vmem((half, 16, lanes), BF16),
         vmem((half, 16, lanes), BF16),
         vmem((SPLIT, 2, lanes), F32),
         vmem((SPLIT, 2, lanes), F32),
-        dma((4,)),
+        dma((8,)),
         dma((2, SPLIT)),
+        dma((2, half)),
+        dma((2, half)),
         dma((2, half)),
         dma((2, half)),
         dma((2, groups)),
         dma((2, 9)),
         dma((2, 9)),
         dma((2, groups)),
+        dma((2, half)),
+        dma((2, half)),
         dma((2, half)),
         dma((2, half)),
         dma((2, SPLIT)),
@@ -432,11 +470,11 @@
             jax.ShapeDtypeStruct(out_grad.shape, BF16),
             jax.ShapeDtypeStruct(expert_ids.shape, F32),
         ),
-        in_specs=[in_vmem] * 4 + [anywhere] * 4,
+        in_specs=[anywhere] * 8,
         out_specs=(in_vmem, in_vmem),
         scratch_shapes=scratch,
         compiler_params=pltpu.CompilerParams(
-            collective_id=0, has_side_effects=True, vmem_limit_bytes=40 * 2**20
+            collective_id=0, has_side_effects=True, vmem_limit_bytes=60 * 2**20
         ),
         name="routed_backward",
     )(out_grad, routing_weight, expert_ids, slot_index, w_gate, w_up, w_down, pre_act)

time: 138 us -> 116 us (0.84)
  Pallas kernels: 128 us -> 113 us
  local copies, waits for them, and re-layouts: 8.31 us -> 1.89 us
    pallas_call x1, Pallas kernels: 128 us -> 113 us  [on_device(): pl.pallas_call(functools.partial(kernel, groups, experts, cap), out_shape...]
    unnamed x18 -> x4, local copies, waits for them, and re-layouts: 8.31 us -> 1.89 us
where the time goes in v2:
time: 116 us
  Pallas kernels  113 us (97%)
  local copies, waits for them, and re-layouts  1.89 us (2%)
    pallas_call x1, Pallas kernels, on_device(): pl.pallas_call(functools.partial(kernel, groups, experts, cap), out_shape...  113 us

profile of v2, /device:TPU:6, one launch (start us, length us, event | category | flops | bytes accessed | tf_op | source)
XLA Modules:
  0.0 115.6 jit_solution(1930691380954959765)
XLA Ops:
  0.6 113.0 %routed_backward.1 = (bf16[2,3584]{1,0:T(2,128)(2,1)}, f32[2,8]{1,0:T(2,128)}) custom-call(bf16[2,3584]{1,0:T(2,128)(2,1)} %grad_hbm.1, bf16[2,8]{1,0:T(2,128)(2,1)} %weight_hbm.1, s32[2,8]{1,0:T(2,128)} %ids_hbm.1, s32[2,8]{1,0:T(2,128)} %slot_hbm.1, bf16[3584,128]{1,0:T(8,128)(2,1)} %wg_hbm.1, bf16[3584,128]{1,0:T(8,128)(2,1)} %wu_hbm.1, ...), custom_call_target="tpu_custom_call" | custom-call | tf_op jit(solution)/shard_map/routed_backward/pallas_call | solution.py:467
  113.7 0.0 copy-start
  113.7 1.3 %copy.12 = bf16[2,3584]{1,0:T(2,128)(2,1)} copy(bf16[2,3584]{1,0:T(2,128)(2,1)} %get-tuple-element.4) | data formatting | bytes 28672
  115.0 0.0 copy-done
  115.0 0.6 copy.13
Async XLA Ops:
  113.7 1.3 %copy-start = (f32[2,8]{1,0:T(2,128)S(1)}, f32[2,8]{1,0:T(2,128)}, u32[]{:S(2)}) copy-start(f32[2,8]{1,0:T(2,128)} %get-tuple-element.5) | copy-start | bytes 196

commit v3 on v2

v3 whole, which is shorter than its diff:
```python
import functools
import jax
import jax.numpy as jnp
from jax import lax
from jax.experimental import pallas as pl
from jax.experimental.pallas import tpu as pltpu
from jax.sharding import PartitionSpec as P

MESH = pl.DeviceIdType.MESH
F32 = jnp.float32
BF16 = jnp.bfloat16
SPLIT = 8
ROWS = 32
CHUNKS = 2
NT = (((1,), (1,)), ((), ()))
TN = (((0,), (0,)), ((), ()))
NN = (((1,), (0,)), ((), ()))


def kernel(
    groups, experts, cap,
    grad_hbm, weight_hbm, ids_hbm, slot_hbm, wg_hbm, wu_hbm, wd_hbm, pre_hbm,
    out_ref, routing_ref,
    grad_ref, weight_ref, ids_ref, slot_ref, wd_cols, wc, pre, stage, block_in,
    block_rows, xbuf, pbuf, wbuf, rbuf, ybuf, dbuf, bsend, brecv, back, gall, gate,
    fbuf, vbuf, ubuf, ubf, gsr, grr, gsl, grl, gnr, gnl, fin, hbuf,
    load_sem, a_sem, ar_sem, al_sem, anr_sem, anl_sem, wd_sem, wc_sem, b_sem, c_sem,
    d_sem, f_sem, gr_sem, gl_sem, gnr_sem, gnl_sem, h_sem,
):
    my_group = lax.axis_index("group")
    my_inner = lax.axis_index("inner")
    le = lax.div(my_inner, SPLIT)
    q = lax.rem(my_inner, SPLIT)
    zp = lax.div(q, 4)
    y = lax.rem(q, 4)
    odd = lax.rem(y, 2)
    width = grad_ref.shape[1]
    part = width // SPLIT
    lanes = xbuf.shape[2]
    last = lanes - 128
    half = experts // 4
    slots = groups * cap

    def window(index):
        return 2 * part * (index // 2) + last * (index % 2)

    def window_at(index):
        return 2 * part * lax.div(index, 2) + last * lax.rem(index, 2)

    def in_block(index):
        return (my_group, le * SPLIT + index)

    def in_ring(step):
        return (my_group, lax.rem(le + step + experts, experts) * SPLIT + q)

    def along_y(step):
        return in_block(zp * 4 + lax.rem(y + step, 4))

    def in_group(step, z):
        return (lax.rem(my_group + step, groups), le * SPLIT + z * 4 + y)

    right, left = in_ring(2), in_ring(-2)
    next_right, next_left = in_ring(1), in_ring(-1)

    def send(src, dst, sems, index, target):
        copy = pltpu.make_async_remote_copy(
            src_ref=src, dst_ref=dst, send_sem=sems.at[0, index],
            recv_sem=sems.at[1, index], device_id=target, device_id_type=MESH,
        )
        copy.start()
        started.append(copy)
        return copy

    started = []
    small = [
        pltpu.make_async_copy(grad_hbm, grad_ref, load_sem.at[0]),
        pltpu.make_async_copy(weight_hbm, weight_ref, load_sem.at[1]),
        pltpu.make_async_copy(ids_hbm, ids_ref, load_sem.at[2]),
        pltpu.make_async_copy(slot_hbm, slot_ref, load_sem.at[3]),
    ]
    for load in small:
        load.start()

    barrier = pltpu.get_barrier_semaphore()
    partners = [in_block(lax.rem(q + d, SPLIT)) for d in range(1, SPLIT)]
    partners += [right, left, next_right, next_left]
    partners += [in_group(d, z) for d in range(1, groups) for z in (zp, 1 - zp)]
    for partner in partners:
        pl.semaphore_signal(barrier, inc=1, device_id=partner, device_id_type=MESH)

    def down_window(z, step):
        at = window_at(z * 4 + lax.rem(y + step, 4))
        return wd_hbm.at[:, pl.ds(pl.multiple_of(at, 128), lanes)]

    def wide_window(ref, z, step):
        at = window_at(z * 4 + lax.rem(y + step, 4))
        return ref.at[pl.ds(pl.multiple_of(at, 128), lanes), :]

    def wide_at(z, which):
        return wc.at[y, z, :, pl.ds(128 * which, 128)]

    loads = [pltpu.make_async_copy(pre_hbm, pre, load_sem.at[4])]
    for z in range(2):
        loads.append(
            pltpu.make_async_copy(down_window(z, 0), wd_cols.at[y, z], load_sem.at[5 + z])
        )
        for which, ref in enumerate((wg_hbm, wu_hbm)):
            loads.append(
                pltpu.make_async_copy(
                    wide_window(ref, z, 0), wide_at(z, which), load_sem.at[7 + 2 * z + which]
                )
            )
    for load in loads:
        load.start()

    for load in small:
        load.wait()
    lane2 = lax.broadcasted_iota(jnp.int32, (2, 128), 1)
    ids = ids_ref[...]
    local = lax.rem(ids, experts).astype(F32)
    row = (lax.div(ids, experts) * ROWS + slot_ref[...]).astype(F32)
    weight = weight_ref[...].astype(F32)
    meta = jnp.zeros((2, 128), F32)
    for k in range(8):
        for at, values in ((0, local), (8, row), (16, weight)):
            meta = jnp.where(lane2 == at + k, values[:, k : k + 1], meta)
    meta_high = pltpu.roll(meta, 64, 1)
    tokens = grad_ref[...].astype(F32)
    for b in range(SPLIT):
        cut = tokens[:, window(b) : window(b) + lanes]
        if b % 2 == 0:
            stage[b, :, 0:last] = cut[:, 0:last]
            stage[b, :, last:lanes] = jnp.where(lane2 < 64, cut[:, last:lanes], meta_high)
        else:
            stage[b, :, 0:128] = jnp.where(lane2 < 64, meta, cut[:, 0:128])
            stage[b, :, 128:lanes] = cut[:, 128:lanes]
    block_in[q] = stage[q]

    pl.semaphore_wait(barrier, len(partners))

    copies = []
    for d in range(1, SPLIT):
        target = lax.rem(q + d, SPLIT)
        copies.append(send(stage.at[target], block_in.at[q], a_sem, d - 1, in_block(target)))

    down_copies, wide_copies = [], []
    for step in (2, 1, 3):
        for z in range(2):
            down_copies.append(
                send(
                    down_window(z, step), wd_cols.at[y, z], wd_sem,
                    (step - 1) * 2 + z, along_y(step),
                )
            )
    for step in (2, 1, 3):
        for z in range(2):
            for which, ref in enumerate((wg_hbm, wu_hbm)):
                wide_copies.append(
                    send(
                        wide_window(ref, z, step), wide_at(z, which), wc_sem,
                        (step - 1) * 4 + z * 2 + which, along_y(step),
                    )
                )
    for copy in copies:
        copy.wait_recv()
    for b in range(SPLIT):
        block_rows[2 * b : 2 * b + 2, :] = block_in[b]
    xbuf[le] = block_rows[...].astype(BF16)

    def block(step):
        return lax.rem(le + step + experts, experts)

    def go(step, sems, index, target):
        return send(xbuf.at[block(step)], xbuf.at[block(step)], sems, index, target)

    lane_key = lax.broadcasted_iota(jnp.int32, (16, groups * ROWS), 1).astype(F32)
    my_local = le.astype(F32)

    def free_lanes(first, final):
        is_odd = jnp.full(first.shape, odd, jnp.int32) == 1
        return jnp.where(is_odd, first.astype(F32), pltpu.roll(final.astype(F32), 64, 1))

    def keys(found):
        return jnp.where(found == my_local, pltpu.roll(found, 120, 1), -1.0)

    def place(at):
        found = free_lanes(xbuf[at, :, 0:128], xbuf[at, :, last:lanes])
        key = keys(found)
        scale = pltpu.roll(found, 112, 1)
        ones = jnp.zeros(lane_key.shape, F32)
        scaled = jnp.zeros(lane_key.shape, F32)
        for k in range(8):
            hit = key[:, k : k + 1] == lane_key
            ones = jnp.where(hit, 1.0, ones)
            scaled = jnp.where(hit, scale[:, k : k + 1], scaled)
        pbuf[at] = ones.astype(BF16)
        wbuf[at] = scaled.astype(BF16)

    to_right = go(0, ar_sem, 0, right)
    to_left = go(0, al_sem, 0, left) if half > 1 else None
    near_right = go(0, anr_sem, 0, next_right)
    near_left = go(0, anl_sem, 0, next_left)
    place(le)
    for k in range(1, half + 1):
        last_right, last_left = near_right, near_left
        if k < half:
            to_left.wait_recv()
            if k < half - 1:
                to_left = go(2 * k, al_sem, k, left)
            near_left = go(2 * k, anl_sem, k, next_left)
        to_right.wait_recv()
        if k < half:
            to_right = go(-2 * k, ar_sem, k, right)
            near_right = go(-2 * k, anr_sem, k, next_right)
            place(block(2 * k))
        last_right.wait_recv()
        last_left.wait_recv()
        for step in (1 - 2 * k, 2 * k - 1, -2 * k):
            place(block(step))
    rows = lax.dot_general(
        pbuf[...].reshape(experts * 16, groups * ROWS),
        xbuf[...].reshape(experts * 16, lanes),
        TN, preferred_element_type=F32,
    )
    rbuf[...] = rows.astype(BF16).reshape(rbuf.shape)

    copies = []
    for d in range(1, groups):
        target = lax.rem(my_group + d, groups)
        for far, z in enumerate((zp, 1 - zp)):
            copies.append(
                send(
                    rbuf.at[target], ybuf.at[zp, my_group], b_sem, d * 2 + far, in_group(d, z)
                )
            )
    copies.append(send(rbuf.at[my_group], ybuf.at[zp, my_group], b_sem, 1, in_group(0, 1 - zp)))
    ybuf[zp, my_group] = rbuf[my_group]
    for copy in copies:
        copy.wait_recv()
    lane_row = lax.broadcasted_iota(jnp.int32, (slots, lanes), 1)
    kept = jnp.logical_and(lane_row >= 64 * odd, lane_row < part + 64 * odd)
    for z in range(2):
        dense = [ybuf[z, s].astype(F32)[0:cap] for s in range(groups)]
        dbuf[z] = jnp.where(kept, jnp.concatenate(dense, axis=0), 0.0).astype(BF16)

    size = slots // CHUNKS

    def rows_of(c):
        return pl.ds(c * size, size)

    for load in loads:
        load.wait()
    for copy in down_copies:
        copy.wait_recv()
    back_copies = []
    for c in range(CHUNKS):
        copies = []
        for step in (2, 1, 3, 0):
            at = lax.rem(y + step, 4)
            value = lax.dot_general(
                dbuf[0, rows_of(c), :], wd_cols[at, 0], NT, preferred_element_type=F32
            ) + lax.dot_general(
                dbuf[1, rows_of(c), :], wd_cols[at, 1], NT, preferred_element_type=F32
            )
            if step == 0:
                back[rows_of(c), :] = value
                continue
            bsend[step, rows_of(c), :] = value.astype(BF16)
            copies.append(
                send(
                    bsend.at[step, rows_of(c)], brecv.at[step, rows_of(c)], c_sem,
                    c * 4 + step, along_y(step),
                )
            )
        back_copies.append(copies)

    wide = []
    for c in range(CHUNKS):
        for copy in back_copies[c]:
            copy.wait_recv()
        rows = rows_of(c)
        proj = back[rows, :]
        for step in range(1, 4):
            proj = proj + brecv[step, rows, :].astype(F32)
        pre_gate = pre[0, rows, :].astype(F32)
        pre_up = pre[1, rows, :].astype(F32)
        sig = jax.nn.sigmoid(pre_gate)
        swish = pre_gate * sig
        gall[y, rows, 0:128] = (
            proj * pre_up * sig * (1.0 + pre_gate * (1.0 - sig))
        ).astype(BF16)
        gall[y, rows, 128:256] = (proj * swish).astype(BF16)
        copies = []
        for step in (2, 1, 3):
            copies.append(
                send(
                    gall.at[y, rows], gall.at[y, rows], d_sem, c * 4 + step, along_y(step)
                )
            )
        wide.append(copies)
        gate[rows, :] = jnp.broadcast_to(
            jnp.sum(swish * pre_up * proj, axis=1, keepdims=True), (size, 128)
        )
    for copy in wide_copies:
        copy.wait_recv()

    def to_group(z, s, sender_z, sender):
        return pltpu.make_async_remote_copy(
            src_ref=fbuf.at[z, s], dst_ref=vbuf.at[sender_z, sender],
            send_sem=f_sem.at[0, z * groups + s],
            recv_sem=f_sem.at[1, sender_z * groups + sender],
            device_id=(s, le * SPLIT + z * 4 + y), device_id_type=MESH,
        )

    def is_here(z, s):
        return jnp.logical_and(my_group == s, zp == z)

    blank = jnp.zeros((ROWS - cap, lanes), F32)
    lane_tile = lax.broadcasted_iota(jnp.int32, (size, 128), 1)
    free_first = jnp.logical_and(lane_tile < 64 * odd, lane_tile < 64)
    free_last = lane_tile >= 64 + 64 * odd
    for c in range(CHUNKS):
        for copy in wide[c]:
            copy.wait_recv()
        rows = rows_of(c)
        for z in range(2):
            value = lax.dot_general(gall[0, rows, :], wc[0, z], NT, preferred_element_type=F32)
            for at in range(1, 4):
                value = value + lax.dot_general(
                    gall[at, rows, :], wc[at, z], NT, preferred_element_type=F32
                )
            terms = gate[rows, :]
            value = jnp.concatenate(
                [
                    jnp.where(free_first, terms, value[:, 0:128]),
                    value[:, 128:last],
                    jnp.where(free_last, terms, value[:, last:lanes]),
                ],
                axis=1,
            )
            for at in range(size // cap):
                s = c * (size // cap) + at
                fbuf[z, s] = jnp.concatenate(
                    [value[at * cap : (at + 1) * cap], blank], axis=0
                ).astype(BF16)

                @pl.when(jnp.logical_not(is_here(z, s)))
                def _():
                    to_group(z, s, zp, my_group).start()

                @pl.when(is_here(z, s))
                def _():
                    vbuf[z, s] = fbuf[z, s]

    for z in range(2):
        for s in range(groups):

            @pl.when(jnp.logical_not(is_here(z, s)))
            def _():
                arriving = to_group(z, s, z, s)
                arriving.wait_recv()
                arriving.wait_send()

    count = experts * 16
    placed = pbuf[...].reshape(count, groups * ROWS)
    scaled = wbuf[...].reshape(count, groups * ROWS)
    row_group = lax.div(lax.broadcasted_iota(jnp.int32, (groups * ROWS, 128), 0), ROWS)
    lane_group = lax.broadcasted_iota(jnp.int32, (groups * ROWS, 128), 1)
    summed, terms = None, None
    for z in range(2):
        arrived = vbuf[z].reshape(groups * ROWS, lanes)
        spread = jnp.where(
            row_group == lane_group,
            free_lanes(arrived[:, 0:128], arrived[:, last:lanes]), 0.0,
        ).astype(BF16)
        more = lax.dot_general(scaled, arrived, NN, preferred_element_type=F32)
        more_terms = lax.dot_general(placed, spread, NN, preferred_element_type=F32)
        summed = more if summed is None else summed + more
        terms = more_terms if terms is None else terms + more_terms
    tokens_in = xbuf[...].reshape(count, lanes)
    key = keys(free_lanes(tokens_in[:, 0:128], tokens_in[:, last:lanes]))
    of_group = jnp.floor(key * (1.0 / ROWS))
    routed = jnp.zeros(key.shape, F32)
    for g in range(groups):
        routed = jnp.where(of_group == g, terms[:, g : g + 1], routed)
    lane_all = lax.broadcasted_iota(jnp.int32, key.shape, 1)
    ubuf[:, :, 0:128] = jnp.where(lane_all < 64 * odd, routed, summed[:, 0:128]).reshape(
        experts, 16, 128
    )
    ubuf[:, :, 128:last] = summed[:, 128:last].reshape(experts, 16, last - 128)
    ubuf[:, :, last:lanes] = jnp.where(
        lane_all >= 64 + 64 * odd, pltpu.roll(routed, 64, 1), summed[:, last:lanes]
    ).reshape(experts, 16, 128)

    ubf[...] = ubuf[...].astype(BF16)
    to_right = send(ubf.at[block(2 * half)], grr.at[0], gr_sem, 0, right)
    to_left = None
    near_right, near_left = [None] * half, [None] * half
    for k in range(half - 1, -1, -1):
        near_left[k] = send(ubf.at[block(-1 - 2 * k)], gnl.at[k], gnl_sem, k, next_left)
        near_right[k] = send(ubf.at[block(1 + 2 * k)], gnr.at[k], gnr_sem, k, next_right)
    for k in range(half - 1, 0, -1):
        at = half - 1 - k
        value = ubuf[block(-2 * k)]
        near_left[k].wait_recv()
        value = value + gnl[k].astype(F32)
        if to_left is not None:
            to_left.wait_recv()
            value = value + grl[at - 1].astype(F32)
        gsl[at] = value.astype(BF16)
        to_left = send(gsl.at[at], grl.at[at], gl_sem, at, left)
        value = ubuf[block(2 * k)]
        near_right[k].wait_recv()
        value = value + gnr[k].astype(F32)
        to_right.wait_recv()
        value = value + grr[at].astype(F32)
        gsr[at] = value.astype(BF16)
        to_right = send(gsr.at[at], grr.at[at + 1], gr_sem, at + 1, right)
    near_right[0].wait_recv()
    near_left[0].wait_recv()
    value = ubuf[le] + gnr[0].astype(F32) + gnl[0].astype(F32)
    if to_left is not None:
        to_left.wait_recv()
        value = value + grl[half - 2].astype(F32)
    to_right.wait_recv()
    value = value + grr[half - 1].astype(F32)

    block_rows[...] = value
    for b in range(SPLIT):
        fin[b] = block_rows[2 * b : 2 * b + 2, :]
    hbuf[q] = fin[q]
    copies = []
    for d in range(1, SPLIT):
        target = lax.rem(q + d, SPLIT)
        copies.append(send(fin.at[target], hbuf.at[q], h_sem, d - 1, in_block(target)))
    for copy in copies:
        copy.wait_recv()
    for m in range(SPLIT // 2):
        even, uneven = hbuf[2 * m], hbuf[2 * m + 1]
        base = 2 * part * m
        out_ref[:, base : base + last] = even[:, 0:last].astype(BF16)
        out_ref[:, base + last : base + lanes] = jnp.where(
            lane2 < 64, even[:, last:lanes], uneven[:, 0:128]
        ).astype(BF16)
        out_ref[:, base + lanes : base + 2 * part] = uneven[:, 128:lanes].astype(BF16)
    routing = pltpu.roll(hbuf[0][:, last:lanes] + hbuf[2][:, last:lanes], 64, 1)
    routing = routing + hbuf[1][:, 0:128] + hbuf[3][:, 0:128]
    routing_ref[...] = routing[:, 0:8]
    for copy in started:
        copy.wait_send()


def on_device(out_grad, routing_weight, expert_ids, slot_index, w_gate, w_up, w_down, pre_act):
    groups = lax.axis_size("group")
    experts = lax.axis_size("inner") // SPLIT
    cap = pre_act.shape[1] // groups
    width = out_grad.shape[1]
    lanes = -(-(width // SPLIT) // 128) * 128
    slots = groups * cap
    hidden = w_down.shape[0]
    half = experts // 4
    vmem = pltpu.VMEM
    dma = pltpu.SemaphoreType.DMA
    scratch = [
        vmem(out_grad.shape, BF16),
        vmem(routing_weight.shape, BF16),
        vmem(expert_ids.shape, jnp.int32),
        vmem(slot_index.shape, jnp.int32),
        vmem((4, 2, hidden, lanes), BF16),
        vmem((4, 2, lanes, 256), BF16),
        vmem((2, slots, hidden), BF16),
        vmem((SPLIT, 2, lanes), F32),
        vmem((SPLIT, 2, lanes), F32),
        vmem((16, lanes), F32),
        vmem((experts, 16, lanes), BF16),
        vmem((experts, 16, groups * ROWS), BF16),
        vmem((experts, 16, groups * ROWS), BF16),
        vmem((groups, ROWS, lanes), BF16),
        vmem((2, groups, ROWS, lanes), BF16),
        vmem((2, slots, lanes), BF16),
        vmem((4, slots, hidden), BF16),
        vmem((4, slots, hidden), BF16),
        vmem((slots, hidden), F32),
        vmem((4, slots, 256), BF16),
        vmem((slots, 128), F32),
        vmem((2, groups, ROWS, lanes), BF16),
        vmem((2, groups, ROWS, lanes), BF16),
        vmem((experts, 16, lanes), F32),
        vmem((experts, 16, lanes), BF16),
        vmem((half, 16, lanes), BF16),
        vmem((half, 16, lanes), BF16),
        vmem((half, 16, lanes), BF16),
        vmem((half, 16, lanes), BF16),
        vmem((half, 16, lanes), BF16),
        vmem((half, 16, lanes), BF16),
        vmem((SPLIT, 2, lanes), F32),
        vmem((SPLIT, 2, lanes), F32),
        dma((11,)),
        dma((2, SPLIT)),
        dma((2, half)),
        dma((2, half)),
        dma((2, half)),
        dma((2, half)),
        dma((2, 6)),
        dma((2, 12)),
        dma((2, 2 * groups)),
        dma((2, 4 * CHUNKS)),
        dma((2, 4 * CHUNKS)),
        dma((2, 2 * groups)),
        dma((2, half)),
        dma((2, half)),
        dma((2, half)),
        dma((2, half)),
        dma((2, SPLIT)),
    ]
    in_vmem = pl.BlockSpec(memory_space=pltpu.VMEM)
    anywhere = pl.BlockSpec(memory_space=pl.ANY)
    return pl.pallas_call(
        functools.partial(kernel, groups, experts, cap),
        out_shape=(
            jax.ShapeDtypeStruct(out_grad.shape, BF16),
            jax.ShapeDtypeStruct(expert_ids.shape, F32),
        ),
        in_specs=[anywhere] * 8,
        out_specs=(in_vmem, in_vmem),
        scratch_shapes=scratch,
        compiler_params=pltpu.CompilerParams(
            collective_id=0, has_side_effects=True, vmem_limit_bytes=60 * 2**20
        ),
        name="routed_backward",
    )(out_grad, routing_weight, expert_ids, slot_index, w_gate, w_up, w_down, pre_act)


def solution(mesh):
    token = P(("group", "inner"), None)
    in_specs = (
        token, token, token, token,
        P(None, ("group", "inner")),
        P(None, ("group", "inner")),
        P(("group", "inner"), None),
        P(None, None, ("group", "inner")),
    )
    return jax.shard_map(
        on_device, mesh=mesh, in_specs=in_specs, out_specs=(token, token), check_vma=False
    )
```

time: 116 us -> 104 us (0.90)
  Pallas kernels: 113 us -> 101 us
    pallas_call x1, Pallas kernels: 113 us -> 101 us  [on_device(): pl.pallas_call(functools.partial(kernel, groups, experts, cap), out_shape...]
where the time goes in v3:
time: 104 us
  Pallas kernels  101 us (97%)
  local copies, waits for them, and re-layouts  1.89 us (2%)
    pallas_call x1, Pallas kernels, on_device(): pl.pallas_call(functools.partial(kernel, groups, experts, cap), out_shape...  101 us

profile of v3, /device:TPU:6, one launch (start us, length us, event | category | flops | bytes accessed | tf_op | source)
XLA Modules:
  0.0 104.0 jit_solution(8818496200596869790)
XLA Ops:
  0.6 101.5 %routed_backward.1 = (bf16[2,3584]{1,0:T(2,128)(2,1)}, f32[2,8]{1,0:T(2,128)}) custom-call(bf16[2,3584]{1,0:T(2,128)(2,1)} %grad_hbm.1, bf16[2,8]{1,0:T(2,128)(2,1)} %weight_hbm.1, s32[2,8]{1,0:T(2,128)} %ids_hbm.1, s32[2,8]{1,0:T(2,128)} %slot_hbm.1, bf16[3584,128]{1,0:T(8,128)(2,1)} %wg_hbm.1, bf16[3584,128]{1,0:T(8,128)(2,1)} %wu_hbm.1, ...), custom_call_target="tpu_custom_call" | custom-call | tf_op jit(solution)/shard_map/routed_backward/pallas_call | solution.py:518
  102.1 0.0 copy-start
  102.1 1.3 %copy.12 = bf16[2,3584]{1,0:T(2,128)(2,1)} copy(bf16[2,3584]{1,0:T(2,128)(2,1)} %get-tuple-element.4) | data formatting | bytes 28672
  103.4 0.0 copy-done
  103.4 0.6 copy.13
Async XLA Ops:
  102.1 1.3 %copy-start = (f32[2,8]{1,0:T(2,128)S(1)}, f32[2,8]{1,0:T(2,128)}, u32[]{:S(2)}) copy-start(f32[2,8]{1,0:T(2,128)} %get-tuple-element.5) | copy-start | bytes 196

commit v4 on v3

--- a/solution.py
+++ b/solution.py
@@ -10,7 +10,6 @@
 F32 = jnp.float32
 BF16 = jnp.bfloat16
 SPLIT = 8
-ROWS = 32
 CHUNKS = 2
 NT = (((1,), (1,)), ((), ()))
 TN = (((0,), (0,)), ((), ()))
@@ -23,9 +22,9 @@
     out_ref, routing_ref,
     grad_ref, weight_ref, ids_ref, slot_ref, wd_cols, wc, pre, stage, block_in,
     block_rows, xbuf, pbuf, wbuf, rbuf, ybuf, dbuf, bsend, brecv, back, gall, gate,
-    fbuf, vbuf, ubuf, ubf, gsr, grr, gsl, grl, gnr, gnl, fin, hbuf,
-    load_sem, a_sem, ar_sem, al_sem, anr_sem, anl_sem, wd_sem, wc_sem, b_sem, c_sem,
-    d_sem, f_sem, gr_sem, gl_sem, gnr_sem, gnl_sem, h_sem,
+    fbuf, vbuf, ubuf, ubf, gr_out, gr_in, gn_in, fin, hbuf,
+    load_sem, a_sem, ar_sem, an_sem, wd_sem, wc_sem, b_sem, c_sem, d_sem, f_sem,
+    gr_sem, gn_sem, h_sem,
 ):
     my_group = lax.axis_index("group")
     my_inner = lax.axis_index("inner")
@@ -38,7 +37,6 @@
     part = width // SPLIT
     lanes = xbuf.shape[2]
     last = lanes - 128
-    half = experts // 4
     slots = groups * cap
 
     def window(index):
@@ -51,7 +49,7 @@
         return (my_group, le * SPLIT + index)
 
     def in_ring(step):
-        return (my_group, lax.rem(le + step + experts, experts) * SPLIT + q)
+        return (my_group, lax.rem(le + step + 2 * experts, experts) * SPLIT + q)
 
     def along_y(step):
         return in_block(zp * 4 + lax.rem(y + step, 4))
@@ -59,8 +57,15 @@
     def in_group(step, z):
         return (lax.rem(my_group + step, groups), le * SPLIT + z * 4 + y)
 
-    right, left = in_ring(2), in_ring(-2)
-    next_right, next_left = in_ring(1), in_ring(-1)
+    routes = {
+        0: [(1, 0), (-1, 0)],
+        -3: [(1, -3), (-1, -3)],
+        3: [(-1, 3), (1, 3)],
+        -6: [(2, -6), (1, -6), (-1, -6)],
+        6: [(-1, 6), (1, 6)],
+    }
+    aside = [route for of in (0, -3, 3, -6, 6) for route in routes[of]]
+    right, left = in_ring(3), in_ring(-3)
 
     def send(src, dst, sems, index, target):
         copy = pltpu.make_async_remote_copy(
@@ -83,7 +88,7 @@
 
     barrier = pltpu.get_barrier_semaphore()
     partners = [in_block(lax.rem(q + d, SPLIT)) for d in range(1, SPLIT)]
-    partners += [right, left, next_right, next_left]
+    partners += [right, left] + [in_ring(step) for step in (1, -1, -2)]
     partners += [in_group(d, z) for d in range(1, groups) for z in (zp, 1 - zp)]
     for partner in partners:
         pl.semaphore_signal(barrier, inc=1, device_id=partner, device_id_type=MESH)
@@ -93,11 +98,12 @@
         return wd_hbm.at[:, pl.ds(pl.multiple_of(at, 128), lanes)]
 
     def wide_window(ref, z, step):
-        at = window_at(z * 4 + lax.rem(y + step, 4))
-        return ref.at[pl.ds(pl.multiple_of(at, 128), lanes), :]
-
-    def wide_at(z, which):
-        return wc.at[y, z, :, pl.ds(128 * which, 128)]
+        index = z * 4 + lax.rem(y + step, 4)
+        return ref.at[pl.ds(pl.multiple_of(part * index, 64), part), :]
+
+    def wide_at(z, which, step):
+        start = pl.multiple_of(64 * lax.rem(y + step, 2), 64)
+        return wc.at[y, z, pl.ds(start, part), pl.ds(128 * which, 128)]
 
     loads = [pltpu.make_async_copy(pre_hbm, pre, load_sem.at[4])]
     for z in range(2):
@@ -107,18 +113,16 @@
         for which, ref in enumerate((wg_hbm, wu_hbm)):
             loads.append(
                 pltpu.make_async_copy(
-                    wide_window(ref, z, 0), wide_at(z, which), load_sem.at[7 + 2 * z + which]
+                    wide_window(ref, z, 0), wide_at(z, which, 0), load_sem.at[7 + 2 * z + which]
                 )
             )
-    for load in loads:
-        load.start()
 
     for load in small:
         load.wait()
     lane2 = lax.broadcasted_iota(jnp.int32, (2, 128), 1)
     ids = ids_ref[...]
     local = lax.rem(ids, experts).astype(F32)
-    row = (lax.div(ids, experts) * ROWS + slot_ref[...]).astype(F32)
+    row = (lax.div(ids, experts) * cap + slot_ref[...]).astype(F32)
     weight = weight_ref[...].astype(F32)
     meta = jnp.zeros((2, 128), F32)
     for k in range(8):
@@ -144,23 +148,32 @@
         copies.append(send(stage.at[target], block_in.at[q], a_sem, d - 1, in_block(target)))
 
     down_copies, wide_copies = [], []
-    for step in (2, 1, 3):
-        for z in range(2):
-            down_copies.append(
-                send(
-                    down_window(z, step), wd_cols.at[y, z], wd_sem,
-                    (step - 1) * 2 + z, along_y(step),
-                )
-            )
-    for step in (2, 1, 3):
-        for z in range(2):
-            for which, ref in enumerate((wg_hbm, wu_hbm)):
-                wide_copies.append(
+
+    def change_down():
+        for step in (2, 1, 3):
+            for z in range(2):
+                down_copies.append(
                     send(
-                        wide_window(ref, z, step), wide_at(z, which), wc_sem,
-                        (step - 1) * 4 + z * 2 + which, along_y(step),
+                        down_window(z, step), wd_cols.at[y, z], wd_sem,
+                        (step - 1) * 2 + z, along_y(step),
                     )
                 )
+
+    def change_wide():
+        for step in (2, 1, 3):
+            for z in range(2):
+                for which, ref in enumerate((wg_hbm, wu_hbm)):
+                    wide_copies.append(
+                        send(
+                            wide_window(ref, z, step), wide_at(z, which, step), wc_sem,
+                            (step - 1) * 4 + z * 2 + which, along_y(step),
+                        )
+                    )
+
+    change_down()
+    change_wide()
+    for load in loads:
+        load.start()
     for copy in copies:
         copy.wait_recv()
     for b in range(SPLIT):
@@ -168,12 +181,23 @@
     xbuf[le] = block_rows[...].astype(BF16)
 
     def block(step):
-        return lax.rem(le + step + experts, experts)
+        return lax.rem(le + step + 2 * experts, experts)
 
     def go(step, sems, index, target):
         return send(xbuf.at[block(step)], xbuf.at[block(step)], sems, index, target)
 
-    lane_key = lax.broadcasted_iota(jnp.int32, (16, groups * ROWS), 1).astype(F32)
+    def go_aside(of):
+        return [
+            (go(of, an_sem, aside.index(route), in_ring(route[0])), of - route[0])
+            for route in routes[of]
+        ]
+
+    def take(arriving):
+        for copy, step in arriving:
+            copy.wait_recv()
+            place(block(step))
+
+    lane_key = lax.broadcasted_iota(jnp.int32, (16, slots), 1).astype(F32)
     my_local = le.astype(F32)
 
     def free_lanes(first, final):
@@ -196,33 +220,42 @@
         pbuf[at] = ones.astype(BF16)
         wbuf[at] = scaled.astype(BF16)
 
-    to_right = go(0, ar_sem, 0, right)
-    to_left = go(0, al_sem, 0, left) if half > 1 else None
-    near_right = go(0, anr_sem, 0, next_right)
-    near_left = go(0, anl_sem, 0, next_left)
+    right_1 = go(0, ar_sem, 0, right)
+    left_1 = go(0, ar_sem, 1, left)
+    arriving = go_aside(0)
     place(le)
-    for k in range(1, half + 1):
-        last_right, last_left = near_right, near_left
-        if k < half:
-            to_left.wait_recv()
-            if k < half - 1:
-                to_left = go(2 * k, al_sem, k, left)
-            near_left = go(2 * k, anl_sem, k, next_left)
-        to_right.wait_recv()
-        if k < half:
-            to_right = go(-2 * k, ar_sem, k, right)
-            near_right = go(-2 * k, anr_sem, k, next_right)
-            place(block(2 * k))
-        last_right.wait_recv()
-        last_left.wait_recv()
-        for step in (1 - 2 * k, 2 * k - 1, -2 * k):
-            place(block(step))
+    take(arriving)
+    right_1.wait_recv()
+    right_2 = go(-3, ar_sem, 2, right)
+    arriving = go_aside(-3)
+    left_1.wait_recv()
+    left_2 = go(3, ar_sem, 3, left)
+    arriving += go_aside(3)
+    place(block(-3))
+    place(block(3))
+    take(arriving)
+    right_2.wait_recv()
+    arriving = go_aside(-6)
+    left_2.wait_recv()
+    arriving += go_aside(6)
+    place(block(-6))
+    place(block(6))
+    take(arriving[1:] + arriving[:1])
+    def fold(value):
+        middle = lanes // 2
+        return jnp.concatenate([value[:, 0:middle], value[:, middle:lanes]], axis=0).astype(BF16)
+
+    def unfold(value):
+        value = value.astype(F32)
+        return jnp.concatenate([value[0:cap], value[cap : 2 * cap]], axis=1)
+
     rows = lax.dot_general(
-        pbuf[...].reshape(experts * 16, groups * ROWS),
+        pbuf[...].reshape(experts * 16, slots),
         xbuf[...].reshape(experts * 16, lanes),
         TN, preferred_element_type=F32,
     )
-    rbuf[...] = rows.astype(BF16).reshape(rbuf.shape)
+    for g in range(groups):
+        rbuf[g] = fold(rows[g * cap : (g + 1) * cap])
 
     copies = []
     for d in range(1, groups):
@@ -240,7 +273,7 @@
     lane_row = lax.broadcasted_iota(jnp.int32, (slots, lanes), 1)
     kept = jnp.logical_and(lane_row >= 64 * odd, lane_row < part + 64 * odd)
     for z in range(2):
-        dense = [ybuf[z, s].astype(F32)[0:cap] for s in range(groups)]
+        dense = [unfold(ybuf[z, s]) for s in range(groups)]
         dbuf[z] = jnp.where(kept, jnp.concatenate(dense, axis=0), 0.0).astype(BF16)
 
     size = slots // CHUNKS
@@ -315,7 +348,6 @@
     def is_here(z, s):
         return jnp.logical_and(my_group == s, zp == z)
 
-    blank = jnp.zeros((ROWS - cap, lanes), F32)
     lane_tile = lax.broadcasted_iota(jnp.int32, (size, 128), 1)
     free_first = jnp.logical_and(lane_tile < 64 * odd, lane_tile < 64)
     free_last = lane_tile >= 64 + 64 * odd
@@ -340,9 +372,7 @@
             )
             for at in range(size // cap):
                 s = c * (size // cap) + at
-                fbuf[z, s] = jnp.concatenate(
-                    [value[at * cap : (at + 1) * cap], blank], axis=0
-                ).astype(BF16)
+                fbuf[z, s] = fold(value[at * cap : (at + 1) * cap])
 
                 @pl.when(jnp.logical_not(is_here(z, s)))
                 def _():
@@ -362,16 +392,17 @@
                 arriving.wait_send()
 
     count = experts * 16
-    placed = pbuf[...].reshape(count, groups * ROWS)
-    scaled = wbuf[...].reshape(count, groups * ROWS)
-    row_group = lax.div(lax.broadcasted_iota(jnp.int32, (groups * ROWS, 128), 0), ROWS)
-    lane_group = lax.broadcasted_iota(jnp.int32, (groups * ROWS, 128), 1)
+    placed = pbuf[...].reshape(count, slots)
+    scaled = wbuf[...].reshape(count, slots)
+    row_group = lax.div(lax.broadcasted_iota(jnp.int32, (slots, 128), 0), cap)
+    lane_group = lax.broadcasted_iota(jnp.int32, (slots, 128), 1)
     summed, terms = None, None
     for z in range(2):
-        arrived = vbuf[z].reshape(groups * ROWS, lanes)
+        whole = jnp.concatenate([unfold(vbuf[z, g]) for g in range(groups)], axis=0)
+        arrived = whole.astype(BF16)
         spread = jnp.where(
             row_group == lane_group,
-            free_lanes(arrived[:, 0:128], arrived[:, last:lanes]), 0.0,
+            free_lanes(whole[:, 0:128], whole[:, last:lanes]), 0.0,
         ).astype(BF16)
         more = lax.dot_general(scaled, arrived, NN, preferred_element_type=F32)
         more_terms = lax.dot_general(placed, spread, NN, preferred_element_type=F32)
@@ -379,7 +410,7 @@
         terms = more_terms if terms is None else terms + more_terms
     tokens_in = xbuf[...].reshape(count, lanes)
     key = keys(free_lanes(tokens_in[:, 0:128], tokens_in[:, last:lanes]))
-    of_group = jnp.floor(key * (1.0 / ROWS))
+    of_group = jnp.floor((key + 0.5) * (1.0 / cap))
     routed = jnp.zeros(key.shape, F32)
     for g in range(groups):
         routed = jnp.where(of_group == g, terms[:, g : g + 1], routed)
@@ -393,37 +424,37 @@
     ).reshape(experts, 16, 128)
 
     ubf[...] = ubuf[...].astype(BF16)
-    to_right = send(ubf.at[block(2 * half)], grr.at[0], gr_sem, 0, right)
-    to_left = None
-    near_right, near_left = [None] * half, [None] * half
-    for k in range(half - 1, -1, -1):
-        near_left[k] = send(ubf.at[block(-1 - 2 * k)], gnl.at[k], gnl_sem, k, next_left)
-        near_right[k] = send(ubf.at[block(1 + 2 * k)], gnr.at[k], gnr_sem, k, next_right)
-    for k in range(half - 1, 0, -1):
-        at = half - 1 - k
-        value = ubuf[block(-2 * k)]
-        near_left[k].wait_recv()
-        value = value + gnl[k].astype(F32)
-        if to_left is not None:
-            to_left.wait_recv()
-            value = value + grl[at - 1].astype(F32)
-        gsl[at] = value.astype(BF16)
-        to_left = send(gsl.at[at], grl.at[at], gl_sem, at, left)
-        value = ubuf[block(2 * k)]
-        near_right[k].wait_recv()
-        value = value + gnr[k].astype(F32)
-        to_right.wait_recv()
-        value = value + grr[at].astype(F32)
-        gsr[at] = value.astype(BF16)
-        to_right = send(gsr.at[at], grr.at[at + 1], gr_sem, at + 1, right)
-    near_right[0].wait_recv()
-    near_left[0].wait_recv()
-    value = ubuf[le] + gnr[0].astype(F32) + gnl[0].astype(F32)
-    if to_left is not None:
-        to_left.wait_recv()
-        value = value + grl[half - 2].astype(F32)
-    to_right.wait_recv()
-    value = value + grr[half - 1].astype(F32)
+    nearer = {}
+    for of in (-6, 6, -3, 3, 0):
+        for route in routes[of]:
+            at = aside.index(route)
+            nearer[route] = send(
+                ubf.at[block(of - route[0])], gn_in.at[at], gn_sem, at, in_ring(-route[0])
+            )
+
+    def with_aside(of):
+        value = ubuf[block(of)]
+        for route in routes[of]:
+            nearer[route].wait_recv()
+            value = value + gn_in[aside.index(route)].astype(F32)
+        return value
+
+    def go_back(value, index, target):
+        gr_out[index] = value.astype(BF16)
+        return send(gr_out.at[index], gr_in.at[index], gr_sem, index, target)
+
+    right_2 = go_back(with_aside(6), 3, right)
+    left_2 = go_back(with_aside(-6), 2, left)
+    value = with_aside(3)
+    right_2.wait_recv()
+    right_1 = go_back(value + gr_in[3].astype(F32), 1, right)
+    value = with_aside(-3)
+    left_2.wait_recv()
+    left_1 = go_back(value + gr_in[2].astype(F32), 0, left)
+    value = with_aside(0)
+    right_1.wait_recv()
+    left_1.wait_recv()
+    value = value + gr_in[0].astype(F32) + gr_in[1].astype(F32)
 
     block_rows[...] = value
     for b in range(SPLIT):
@@ -458,7 +489,6 @@
     lanes = -(-(width // SPLIT) // 128) * 128
     slots = groups * cap
     hidden = w_down.shape[0]
-    half = experts // 4
     vmem = pltpu.VMEM
     dma = pltpu.SemaphoreType.DMA
     scratch = [
@@ -473,44 +503,37 @@
         vmem((SPLIT, 2, lanes), F32),
         vmem((16, lanes), F32),
         vmem((experts, 16, lanes), BF16),
-        vmem((experts, 16, groups * ROWS), BF16),
-        vmem((experts, 16, groups * ROWS), BF16),
-        vmem((groups, ROWS, lanes), BF16),
-        vmem((2, groups, ROWS, lanes), BF16),
+        vmem((experts, 16, slots), BF16),
+        vmem((experts, 16, slots), BF16),
+        vmem((groups, 2 * cap, lanes // 2), BF16),
+        vmem((2, groups, 2 * cap, lanes // 2), BF16),
         vmem((2, slots, lanes), BF16),
         vmem((4, slots, hidden), BF16),
         vmem((4, slots, hidden), BF16),
         vmem((slots, hidden), F32),
         vmem((4, slots, 256), BF16),
         vmem((slots, 128), F32),
-        vmem((2, groups, ROWS, lanes), BF16),
-        vmem((2, groups, ROWS, lanes), BF16),
+        vmem((2, groups, 2 * cap, lanes // 2), BF16),
+        vmem((2, groups, 2 * cap, lanes // 2), BF16),
         vmem((experts, 16, lanes), F32),
         vmem((experts, 16, lanes), BF16),
-        vmem((half, 16, lanes), BF16),
-        vmem((half, 16, lanes), BF16),
-        vmem((half, 16, lanes), BF16),
-        vmem((half, 16, lanes), BF16),
-        vmem((half, 16, lanes), BF16),
-        vmem((half, 16, lanes), BF16),
+        vmem((4, 16, lanes), BF16),
+        vmem((4, 16, lanes), BF16),
+        vmem((11, 16, lanes), BF16),
         vmem((SPLIT, 2, lanes), F32),
         vmem((SPLIT, 2, lanes), F32),
         dma((11,)),
         dma((2, SPLIT)),
-        dma((2, half)),
-        dma((2, half)),
-        dma((2, half)),
-        dma((2, half)),
+        dma((2, 4)),
+        dma((2, 11)),
         dma((2, 6)),
         dma((2, 12)),
         dma((2, 2 * groups)),
         dma((2, 4 * CHUNKS)),
         dma((2, 4 * CHUNKS)),
         dma((2, 2 * groups)),
-        dma((2, half)),
-        dma((2, half)),
-        dma((2, half)),
-        dma((2, half)),
+        dma((2, 4)),
+        dma((2, 11)),
         dma((2, SPLIT)),
     ]
     in_vmem = pl.BlockSpec(memory_space=pltpu.VMEM)

time: 104 us -> 99.9 us (0.961)
  Pallas kernels: 101 us -> 97.1 us
    pallas_call x1, Pallas kernels: 101 us -> 97.1 us  [on_device(): pl.pallas_call(functools.partial(kernel, groups, experts, cap), out_shape...]
where the time goes in v4:
time: 99.9 us; the launch traced here: 99.6 us
  Pallas kernels  97.1 us (97%)
  local copies, waits for them, and re-layouts  1.89 us (2%)
    pallas_call x1, Pallas kernels, on_device(): pl.pallas_call(functools.partial(kernel, groups, experts, cap), out_shape...  97.1 us

profile of v4, /device:TPU:6, one launch (start us, length us, event | category | flops | bytes accessed | tf_op | source)
XLA Modules:
  0.0 99.6 jit_solution(12688483723140118746)
XLA Ops:
  0.6 97.1 %routed_backward.1 = (bf16[2,3584]{1,0:T(2,128)(2,1)}, f32[2,8]{1,0:T(2,128)}) custom-call(bf16[2,3584]{1,0:T(2,128)(2,1)} %grad_hbm.1, bf16[2,8]{1,0:T(2,128)(2,1)} %weight_hbm.1, s32[2,8]{1,0:T(2,128)} %ids_hbm.1, s32[2,8]{1,0:T(2,128)} %slot_hbm.1, bf16[3584,128]{1,0:T(8,128)(2,1)} %wg_hbm.1, bf16[3584,128]{1,0:T(8,128)(2,1)} %wu_hbm.1, ...), custom_call_target="tpu_custom_call" | custom-call | tf_op jit(solution)/shard_map/routed_backward/pallas_call | solution.py:541
  97.7 0.0 copy-start
  97.8 1.3 %copy.12 = bf16[2,3584]{1,0:T(2,128)(2,1)} copy(bf16[2,3584]{1,0:T(2,128)(2,1)} %get-tuple-element.4) | data formatting | bytes 28672
  99.1 0.0 copy-done
  99.1 0.6 copy.13
Async XLA Ops:
  97.7 1.3 %copy-start = (f32[2,8]{1,0:T(2,128)S(1)}, f32[2,8]{1,0:T(2,128)}, u32[]{:S(2)}) copy-start(f32[2,8]{1,0:T(2,128)} %get-tuple-element.5) | copy-start | bytes 196

commit v5 on v4

--- a/solution.py
+++ b/solution.py
@@ -10,7 +10,7 @@
 F32 = jnp.float32
 BF16 = jnp.bfloat16
 SPLIT = 8
-CHUNKS = 2
+CHUNKS = 4
 NT = (((1,), (1,)), ((), ()))
 TN = (((0,), (0,)), ((), ()))
 NN = (((1,), (0,)), ((), ()))

time: 99.9 us -> 101 us (1.011)
  no operation moved by 1% of the time
where the time goes in v5:
time: 101 us; the launch traced here: 100 us
  Pallas kernels  97.8 us (97%)
  local copies, waits for them, and re-layouts  1.89 us (2%)
    pallas_call x1, Pallas kernels, on_device(): pl.pallas_call(functools.partial(kernel, groups, experts, cap), out_shape...  97.8 us

profile of v5, /device:TPU:6, one launch (start us, length us, event | category | flops | bytes accessed | tf_op | source)
XLA Modules:
  0.0 100.4 jit_solution(18030136770539164214)
XLA Ops:
  0.6 97.8 %routed_backward.1 = (bf16[2,3584]{1,0:T(2,128)(2,1)}, f32[2,8]{1,0:T(2,128)}) custom-call(bf16[2,3584]{1,0:T(2,128)(2,1)} %grad_hbm.1, bf16[2,8]{1,0:T(2,128)(2,1)} %weight_hbm.1, s32[2,8]{1,0:T(2,128)} %ids_hbm.1, s32[2,8]{1,0:T(2,128)} %slot_hbm.1, bf16[3584,128]{1,0:T(8,128)(2,1)} %wg_hbm.1, bf16[3584,128]{1,0:T(8,128)(2,1)} %wu_hbm.1, ...), custom_call_target="tpu_custom_call" | custom-call | tf_op jit(solution)/shard_map/routed_backward/pallas_call | solution.py:541
  98.5 0.0 copy-start
  98.5 1.3 %copy.12 = bf16[2,3584]{1,0:T(2,128)(2,1)} copy(bf16[2,3584]{1,0:T(2,128)(2,1)} %get-tuple-element.4) | data formatting | bytes 28672
  99.8 0.0 copy-done
  99.8 0.6 copy.13
Async XLA Ops:
  98.5 1.3 %copy-start = (f32[2,8]{1,0:T(2,128)S(1)}, f32[2,8]{1,0:T(2,128)}, u32[]{:S(2)}) copy-start(f32[2,8]{1,0:T(2,128)} %get-tuple-element.5) | copy-start | bytes 196
